TPU v7x, 256 devices: a whole 4x4x8 slice. The times are simulated.
256 devices in a mesh: pipe: 16 (over x_hi, z), seq: 2 (over x_lo), tensor: 8 (over y, core).
Axes of the slice: x: 4 (x_hi: 2, x_lo: 2; x = x_hi * 2 + x_lo), y: 4, z: 8, core: 2. Of those that a mesh axis runs over, the one named last changes fastest.
Arguments:
- ffn_input: bfloat16 [1024, 8192], P(None, ('seq', 'tensor')), may hold values from -6 to 6
- w_gate_up: bfloat16 [2, 8192, 14336], P(None, ('seq', 'tensor'), 'pipe'), may hold values from -0.0625 to 0.0625
- w_down: bfloat16 [14336, 8192], P('pipe', ('seq', 'tensor')), may hold values from -0.046875 to 0.046875
- stream: bfloat16 [1024, 8192], P('pipe', ('seq', 'tensor')), may hold values from -6 to 6
- attn_gain: float32 [8192], replicated, may hold values from 0.1 to 1.9
- w_query: bfloat16 [8192, 8, 4, 128], P(None, 'tensor', 'seq'), may hold values from -0.0625 to 0.0625
- w_kv: bfloat16 [8192, 2, 8, 128], P(None, None, 'tensor'), may hold values from -0.0625 to 0.0625
- cache_kv: bfloat16 [16, 2, 1024, 8, 128], P('pipe', None, None, 'tensor'), may hold values from -62 to 62
- cache_len: int32 [16], P('pipe'), may hold values from 1 to 1024, as said below
Outputs:
- stream_out: bfloat16 [1024, 8192], P('pipe', ('seq', 'tensor'))
- attended: bfloat16 [1024, 8, 4, 128], P('pipe', 'tensor', 'seq')
Inputs may be any that keep to these rules, and one draw needn't show every extreme that they name: Each request's cache holds valid entries at its first cache_len positions; in every draw some request fills all 1024 positions.
All inputs are finite; a program needn't handle non-finite values.
Results may differ from a plain program's by a relative error of at most 0.034.
Values may be sent and summed in bfloat16 or wider, within the bound.
A program may use at most 128 MiB of HBM per device.

v0:
```python
import math

import jax
import jax.numpy as jnp
from jax import lax
from jax.sharding import PartitionSpec as P

norm_eps = 1e-05
rope_theta = 500000.0


def rotate(values, cosine, sine_part):
    half_dim = values.shape[-1] // 2
    first_half = values[..., :half_dim]
    second_half = values[..., half_dim:]
    return jnp.concatenate(
        [
            first_half * cosine - second_half * sine_part,
            second_half * cosine + first_half * sine_part,
        ],
        axis=-1,
    )


def attend(queries, new_keys, new_vals, cache_keys, cache_vals, cache_len):
    head_scale = queries.shape[-1] ** (-0.5)
    cache_count = cache_keys.shape[1]
    span_len = queries.shape[1]
    cache_scores = (
        jnp.einsum("rckgh,rlkh->rkgcl", queries, cache_keys, preferred_element_type=jnp.float32)
        * head_scale
    )
    own_scores = (
        jnp.einsum("rckgh,rjkh->rkgcj", queries, new_keys, preferred_element_type=jnp.float32)
        * head_scale
    )
    cache_valid = (jnp.arange(cache_count, dtype=jnp.int32)[None, :] < cache_len[:, None])[
        :, None, None, None, :
    ]
    causal = (
        jnp.arange(span_len, dtype=jnp.int32)[None, :]
        <= jnp.arange(span_len, dtype=jnp.int32)[:, None]
    )[None, None, None, :, :]
    cache_scores = jnp.where(cache_valid, cache_scores, -1e30)
    own_scores = jnp.where(causal, own_scores, -1e30)
    row_max = jnp.maximum(
        jnp.max(cache_scores, axis=-1, keepdims=True), jnp.max(own_scores, axis=-1, keepdims=True)
    )
    cache_exp = jnp.exp(cache_scores - row_max)
    own_exp = jnp.exp(own_scores - row_max)
    denominator = jnp.sum(cache_exp, axis=-1, keepdims=True) + jnp.sum(
        own_exp, axis=-1, keepdims=True
    )
    cache_w = (cache_exp / denominator).astype(jnp.bfloat16)
    own_w = (own_exp / denominator).astype(jnp.bfloat16)
    result = jnp.einsum(
        "rkgcl,rlkh->rckgh", cache_w, cache_vals, preferred_element_type=jnp.float32
    )
    result = result + jnp.einsum(
        "rkgcj,rjkh->rckgh", own_w, new_vals, preferred_element_type=jnp.float32
    )
    return result.astype(jnp.bfloat16)


def body(ffn_input, w_gate_up, w_down, stream, attn_gain, w_query, w_kv, cache_kv, cache_len):
    ff_width = w_gate_up.shape[2]
    token_count = ffn_input.shape[0]
    row_block = ffn_input
    product = jnp.einsum("td,edf->tef", row_block, w_gate_up, preferred_element_type=jnp.float32)
    summed = lax.psum(product.reshape(token_count, 2 * ff_width), ("seq", "tensor"))
    hidden = (jax.nn.silu(summed[:, :ff_width]) * summed[:, ff_width:]).astype(jnp.bfloat16)
    group_rows = stream.shape[0]
    row_block = hidden
    ffn_out = lax.psum_scatter(
        jnp.dot(row_block, w_down, preferred_element_type=jnp.float32),
        "pipe",
        scatter_dimension=0,
        tiled=True,
    )
    mixed = (stream.astype(jnp.float32) + ffn_out).astype(jnp.bfloat16)
    full_rows = lax.all_gather(mixed, ("seq", "tensor"), axis=1, tiled=True)
    wide = full_rows.astype(jnp.float32)
    mean_sq = jnp.mean(wide * wide, axis=1, keepdims=True)
    normed = (wide * lax.rsqrt(mean_sq + norm_eps) * attn_gain).astype(jnp.bfloat16)
    queries = jnp.einsum("td,dkgh->tkgh", normed, w_query, preferred_element_type=jnp.float32)
    keyval = jnp.einsum("td,dekh->tekh", normed, w_kv, preferred_element_type=jnp.float32)
    requests = cache_len.shape[0]
    span_len = group_rows // requests
    head_dim = w_query.shape[3]
    half_dim = head_dim // 2
    positions = (
        (cache_len[:, None] + jnp.arange(span_len, dtype=jnp.int32)[None, :])
        .reshape(group_rows)
        .astype(jnp.float32)
    )
    inv_freq = jnp.exp(
        jnp.arange(half_dim, dtype=jnp.float32) * (-2.0 * math.log(rope_theta) / head_dim)
    )
    angles = positions[:, None] * inv_freq[None, :]
    cosine = jnp.cos(angles)
    sine_part = jnp.sin(angles)
    q_rot = rotate(queries, cosine[:, None, None, :], sine_part[:, None, None, :]).astype(
        jnp.bfloat16
    )
    k_new = rotate(keyval[:, 0], cosine[:, None, :], sine_part[:, None, :]).astype(jnp.bfloat16)
    v_new = keyval[:, 1].astype(jnp.bfloat16)
    kv_local = w_query.shape[1]
    group_local = w_query.shape[2]
    q_rot = q_rot.reshape(requests, span_len, kv_local, group_local, head_dim)
    k_new = k_new.reshape(requests, span_len, kv_local, head_dim)
    v_new = v_new.reshape(requests, span_len, kv_local, head_dim)
    attended = attend(q_rot, k_new, v_new, cache_kv[:, 0], cache_kv[:, 1], cache_len)
    return (mixed, attended.reshape(group_rows, kv_local, group_local, head_dim))


def solution(mesh):
    in_specs = (
        P(None, ("seq", "tensor")),
        P(None, ("seq", "tensor"), "pipe"),
        P("pipe", ("seq", "tensor")),
        P("pipe", ("seq", "tensor")),
        P(),
        P(None, "tensor", "seq", None),
        P(None, None, "tensor", None),
        P("pipe", None, None, "tensor", None),
        P("pipe"),
    )
    out_specs = (P("pipe", ("seq", "tensor")), P("pipe", "tensor", "seq", None))
    return jax.shard_map(body, mesh=mesh, in_specs=in_specs, out_specs=out_specs, check_vma=False)
```

profile of v0, /device:TPU:1, one launch (start us, length us, event | category | flops | bytes accessed | tf_op | source)
XLA Modules:
  0.0 425.3 jit_solution(16459439907249665334)
XLA Ops:
  7.2 0.0 copy-start
  7.2 0.0 all-reduce.2.cloned.1.call-start
  7.2 1.4 copy-done
  8.7 6.4 %fusion.24 = f32[1024,2,896]{0,2,1:T(8,128)} fusion(bf16[2,512,896]{2,1,0:T(8,128)(2,1)S(1)} %copy-done, bf16[1024,512]{1,0:T(8,128)(2,1)} %param.9), kind=kOutput, calls=%fused_computation.26 | convolution fusion | flops 1879048192 | bytes 10223616 | tf_op jit(solution)/shard_map/td,edf->tef/dot_general | solution.py:69
  15.0 0.0 copy-start.5
  15.0 0.0 all-reduce.2.cloned.1.call-update
  15.1 0.0 copy-start.3
  15.1 0.0 copy-start.6
  15.1 0.0 reduce-scatter.2.cloned.1.call-start
  15.1 147.2 %all-reduce.2.cloned.1.call-done = f32[1024,1792]{0,1:T(8,128)} async-done(((f32[1024,1792]{0,1:T(8,128)}), f32[1024,1792]{0,1:T(8,128)}) %all-reduce.2.cloned.1.call-update) | async-done | bytes 7340048 | tf_op jit(solution)/shard_map/psum | solution.py:70
  162.4 0.0 copy-done.5
  162.4 5.9 %fusion.8 = f32[1024,512]{1,0:T(8,128)} fusion(bf16[896,512]{1,0:T(8,128)(2,1)S(1)} %copy-done.5, f32[1024,1792]{0,1:T(8,128)} %all-reduce.2.cloned.1.call-done), kind=kOutput, calls=%fused_computation.11 | convolution fusion | flops 945029120 | bytes 10354688 | tf_op jit(solution)/shard_map/dot_general | solution.py:75
  168.2 0.0 reduce-scatter.2.cloned.1.call-update
  168.3 0.0 all-gather.2.cloned.1.call-start
  168.3 200.8 %reduce-scatter.2.cloned.1.call-done = f32[64,512]{1,0:T(8,128)} async-done(((f32[1024,512]{1,0:T(8,128)}), f32[64,512]{1,0:T(8,128)}) %reduce-scatter.2.cloned.1.call-update) | async-done | bytes 131088 | tf_op jit(solution)/shard_map/reduce_scatter | solution.py:74
  369.2 0.0 copy-done.3
  369.2 1.5 add_convert_fusion
  370.7 0.0 all-gather.2.cloned.1.call-update
  371.4 0.2 multiply_cosine_fusion.1
  371.6 38.3 %all-gather.2.cloned.1.call-done = bf16[64,8192]{1,0:T(8,128)(2,1)} async-done(((bf16[64,512]{1,0:T(8,128)(2,1)}), bf16[64,8192]{1,0:T(8,128)(2,1)}) %all-gather.2.cloned.1.call-update) | async-done | bytes 1048592 | tf_op jit(solution)/shard_map/all_gather | solution.py:81
  410.0 1.5 fusion.5
  411.5 0.0 copy-start.1
  411.5 0.0 copy-start.4
  411.5 0.0 copy-done.6
  411.6 3.6 fusion.16
  415.1 0.0 copy-start.2
  415.2 0.2 fusion.52
  415.4 0.0 copy-done.1
  415.4 0.2 copy-done.4
  415.6 0.9 fusion.13
  416.5 0.1 fusion.43
  416.6 0.0 copy-done.2
  416.6 0.4 fusion.56
  417.0 0.3 fusion.57
  417.3 0.2 fusion.28
  417.6 0.3 convolution_bitcast_fusion
  417.9 0.2 fusion.22
  418.1 0.6 copy.15
  (9 shorter events, 0.1 us)
Async XLA Ops:
  7.2 1.5 copy-start
  7.2 155.2 %all-reduce.2.cloned.1.call-start = ((), (), s32[]{:S(2)}) async-start(), calls=%async_computation.1 | async-start | bytes 14680064 | tf_op jit(solution)/shard_map/psum | solution.py:70
  15.0 147.3 %copy-start.5 = (bf16[896,512]{1,0:T(8,128)(2,1)S(1)}, bf16[896,512]{1,0:T(8,128)(2,1)}, u32[]{:S(2)}) copy-start(bf16[896,512]{1,0:T(8,128)(2,1)} %param.11) | copy-start | bytes 2752516
  15.1 354.1 %copy-start.3 = (bf16[64,512]{1,0:T(8,128)(2,1)S(1)}, bf16[64,512]{1,0:T(8,128)(2,1)}, u32[]{:S(2)}) copy-start(bf16[64,512]{1,0:T(8,128)(2,1)} %param.12) | copy-start | bytes 196612
  15.1 396.5 %copy-start.6 = (f32[8192]{0:T(1024)S(1)}, f32[8192]{0:T(1024)}, u32[]{:S(2)}) copy-start(f32[8192]{0:T(1024)} %param.13) | copy-start | bytes 98308
  15.1 354.1 %reduce-scatter.2.cloned.1.call-start = ((), (), s32[]{:S(2)}) async-start(), calls=%async_computation.2 | async-start | bytes 2228224 | tf_op jit(solution)/shard_map/reduce_scatter | solution.py:74
  168.3 241.7 %all-gather.2.cloned.1.call-start = ((), (), s32[]{:S(2)}) async-start(), calls=%async_computation.3 | async-start | bytes 1114112 | tf_op jit(solution)/shard_map/all_gather | solution.py:81
  411.5 3.8 copy-start.1
  411.5 4.1 copy-start.4
  415.1 1.5 copy-start.2
Sparse Core Ops, SparseCore 0:
  15.2 147.1 all-reduce.1
  168.4 200.7 reduce-scatter.1
  371.5 38.3 all-gather.1
where the time goes:
time: 425 us
  waiting for transfers between devices  386 us (91%)
  matrix products  17.9 us (4%)
  between operations  14.6 us (3%)
    reduce_scatter x1, waiting for transfers between devices, body(): lax.psum_scatter(jnp.dot(row_block, w_down, preferred_element_type=jnp.fl...  201 us
    psum x1, waiting for transfers between devices, body(): lax.psum(product.reshape(token_count, 2 * ff_width), ('seq', 'tensor'))  147 us
    all_gather x1, waiting for transfers between devices, body(): full_rows = lax.all_gather(mixed, ('seq', 'tensor'), axis=1, tiled=True)  38.3 us
  transfers between devices with their start and end apart: 3, of which 3 were waited for; matrix products, arithmetic and copies ran while one was open for 0% of the time, Pallas kernels for 0%

commit v1 on v0

--- a/solution.py
+++ b/solution.py
@@ -3,10 +3,20 @@
 import jax
 import jax.numpy as jnp
 from jax import lax
+from jax.experimental import pallas as pl
+from jax.experimental.pallas import tpu as pltpu
 from jax.sharding import PartitionSpec as P
 
 norm_eps = 1e-05
 rope_theta = 500000.0
+MESH = pl.DeviceIdType.MESH
+BF = jnp.bfloat16
+F32 = jnp.float32
+
+CHUNKS = 4
+ROWS = 16
+CHIPS = 8
+OFFSETS = [(a, b) for a in range(2) for b in range(4)][1:]
 
 
 def rotate(values, cosine, sine_part):
@@ -62,23 +72,233 @@
     return result.astype(jnp.bfloat16)
 
 
+def wait_bytes(ref, sem):
+    pltpu.make_async_copy(ref, ref, sem).wait()
+
+
+def ffn_kernel(
+    x_hbm,
+    wgu_hbm,
+    wd_hbm,
+    stream_ref,
+    mixed_ref,
+    full_ref,
+    x_v,
+    wgu_v,
+    wd_v,
+    core_send,
+    core_recv,
+    rs_send,
+    rs_recv,
+    hid_own,
+    hid_all,
+    z_send,
+    z_recv,
+    xh_send,
+    xh_recv,
+    xh_own,
+    full_all,
+    load_sem,
+    send_sem,
+    recv_sem,
+):
+    p = lax.axis_index("pipe")
+    s = lax.axis_index("seq")
+    t = lax.axis_index("tensor")
+    xh, z = p // 8, p % 8
+    y, core = t // 2, t % 2
+    k = s * 4 + y
+    sibling = (p, s, y * 2 + 1 - core)
+
+    loads = [
+        pltpu.make_async_copy(src, dst, load_sem.at[i])
+        for i, (src, dst) in enumerate(((x_hbm, x_v), (wgu_hbm, wgu_v), (wd_hbm, wd_v)))
+    ]
+    for load in loads:
+        load.start()
+
+    def group_peer(da, db):
+        s2 = (s + da) % 2
+        y2 = (y + db) % 4
+        return s2 * 4 + y2, (p, s2, y2 * 2 + core)
+
+    def z_peer(dz):
+        z2 = (z + dz) % 8
+        return z2, (xh * 8 + z2, s, t)
+
+    x_peer = ((1 - xh) * 8 + z, s, t)
+
+    barrier = pltpu.get_barrier_semaphore()
+    everyone = [sibling, x_peer]
+    everyone += [group_peer(*o)[1] for o in OFFSETS]
+    everyone += [z_peer(dz)[1] for dz in range(1, 8)]
+    for peer in everyone:
+        pl.semaphore_signal(barrier, inc=1, device_id=peer, device_id_type=MESH)
+
+    def send(src, dst, kind, c, peer):
+        pltpu.make_async_remote_copy(
+            src_ref=src,
+            dst_ref=dst,
+            send_sem=send_sem.at[kind, c],
+            recv_sem=recv_sem.at[kind, c],
+            device_id=peer,
+            device_id_type=MESH,
+        ).start()
+
+    def gate_up(rows, c):
+        left = x_v[:, rows, pl.ds(c * ROWS, ROWS), :].reshape(CHIPS * ROWS, 512)
+        return [
+            jnp.dot(left, wgu_v[e], preferred_element_type=F32).reshape(CHIPS, ROWS, 896)
+            for e in range(2)
+        ]
+
+    def stage_a(c):
+        for e, part in enumerate(gate_up(1 - core, c)):
+            core_send[c, :, :, e * 896 : (e + 1) * 896] = part.astype(BF)
+        send(core_send.at[c], core_recv.at[c], 0, c, sibling)
+
+    def stage_b(c):
+        parts = gate_up(core, c)
+        wait_bytes(core_recv.at[c], recv_sem.at[0, c])
+        for e, part in enumerate(parts):
+            cols = slice(e * 896, (e + 1) * 896)
+            rs_send[c, :, :, cols] = (part + core_recv[c, :, :, cols].astype(F32)).astype(BF)
+        for j, o in enumerate(OFFSETS):
+            k2, peer = group_peer(*o)
+            send(rs_send.at[c, k2], rs_recv.at[c, j], 1, c, peer)
+
+    def stage_c(c):
+        wait_bytes(rs_recv.at[c], recv_sem.at[1, c])
+        total = rs_send[c, k].astype(F32)
+        for j in range(7):
+            total = total + rs_recv[c, j].astype(F32)
+        gate, up = total[:, :896], total[:, 896:]
+        hidden = (jax.nn.silu(gate) * up).astype(BF)
+        hid_own[c] = hidden
+        hid_all[c, k, core] = hidden
+        for o in OFFSETS:
+            _, peer = group_peer(*o)
+            send(hid_own.at[c], hid_all.at[c, k, core], 2, c, peer)
+
+    def stage_d(c):
+        wait_bytes(hid_all.at[c, 0:7, 0], recv_sem.at[2, c])
+        send(hid_all.at[c, :, core], hid_all.at[c, :, core], 3, c, sibling)
+
+    def stage_e(c):
+        wait_bytes(hid_all.at[c, :, 0], recv_sem.at[3, c])
+        left = hid_all[c].reshape(2 * CHIPS * ROWS, 896)
+        z_send[c] = (
+            jnp.dot(left, wd_v[...], preferred_element_type=F32).astype(BF).reshape(2, 8, ROWS, 512)
+        )
+        for dz in range(1, 8):
+            z2, peer = z_peer(dz)
+            send(z_send.at[c, :, z2], z_recv.at[c, dz - 1], 4, c, peer)
+
+    def stage_f(c):
+        wait_bytes(z_recv.at[c], recv_sem.at[4, c])
+
+        def total(a):
+            value = z_send[c, a, z].astype(F32)
+            for j in range(7):
+                value = value + z_recv[c, j, a].astype(F32)
+            return value
+
+        xh_send[c] = total(1 - xh).astype(BF)
+        send(xh_send.at[c], xh_recv.at[c], 5, c, x_peer)
+        xh_own[c] = total(xh)
+
+    def stage_g(c):
+        wait_bytes(xh_recv.at[c], recv_sem.at[5, c])
+        rows = slice(c * ROWS, (c + 1) * ROWS)
+        ffn_out = xh_own[c] + xh_recv[c].astype(F32)
+        mixed = (stream_ref[rows, :].astype(F32) + ffn_out).astype(BF)
+        mixed_ref[rows, :] = mixed
+        full_all[c, k, core] = mixed
+        for o in OFFSETS:
+            _, peer = group_peer(*o)
+            send(mixed_ref.at[rows], full_all.at[c, k, core], 6, c, peer)
+
+    def stage_h(c):
+        wait_bytes(full_all.at[c, 0:7, 0], recv_sem.at[6, c])
+        send(full_all.at[c, :, core], full_all.at[c, :, core], 7, c, sibling)
+
+    def stage_i(c):
+        wait_bytes(full_all.at[c, :, 0], recv_sem.at[7, c])
+        rows = slice(c * ROWS, (c + 1) * ROWS)
+        for m in range(16):
+            full_ref[rows, m * 512 : (m + 1) * 512] = full_all[c, m // 2, m % 2]
+
+    loads[0].wait()
+    loads[1].wait()
+    pl.semaphore_wait(barrier, len(everyone))
+    stages = dict(
+        a=stage_a, b=stage_b, c=stage_c, d=stage_d, e=stage_e, f=stage_f, g=stage_g, h=stage_h, i=stage_i
+    )
+    order = (
+        "a0", "a1", "b0", "a2", "b1", "a3", "b2", "b3", "c0",
+        "c1", "d0", "c2", "d1", "e0", "c3", "d2", "e1", "f0",
+        "d3", "e2", "f1", "g0", "e3", "f2", "g1", "h0", "f3",
+        "g2", "h1", "i0", "g3", "h2", "i1", "h3", "i2", "i3",
+    )
+    waited = False
+    for step in order:
+        if step[0] == "e" and not waited:
+            loads[2].wait()
+            waited = True
+        stages[step[0]](int(step[1]))
+
+    for c in range(CHUNKS):
+        wait_bytes(core_send.at[c], send_sem.at[0, c])
+        wait_bytes(rs_recv.at[c], send_sem.at[1, c])
+        wait_bytes(hid_all.at[c, 0:7, 0], send_sem.at[2, c])
+        wait_bytes(hid_all.at[c, :, 0], send_sem.at[3, c])
+        wait_bytes(z_recv.at[c], send_sem.at[4, c])
+        wait_bytes(xh_send.at[c], send_sem.at[5, c])
+        wait_bytes(full_all.at[c, 0:7, 0], send_sem.at[6, c])
+        wait_bytes(full_all.at[c, :, 0], send_sem.at[7, c])
+
+
+def ffn_block(ffn_input, w_gate_up, w_down, stream):
+    vmem = pl.BlockSpec(memory_space=pltpu.VMEM)
+    hbm = pl.BlockSpec(memory_space=pl.ANY)
+    return pl.pallas_call(
+        ffn_kernel,
+        out_shape=(
+            jax.ShapeDtypeStruct((64, 512), BF),
+            jax.ShapeDtypeStruct((64, 8192), BF),
+        ),
+        in_specs=[hbm, hbm, hbm, vmem],
+        out_specs=(vmem, vmem),
+        scratch_shapes=[
+            pltpu.VMEM((CHIPS, 2, 64, 512), BF),
+            pltpu.VMEM((2, 512, 896), BF),
+            pltpu.VMEM((896, 512), BF),
+            pltpu.VMEM((CHUNKS, CHIPS, ROWS, 1792), BF),
+            pltpu.VMEM((CHUNKS, CHIPS, ROWS, 1792), BF),
+            pltpu.VMEM((CHUNKS, CHIPS, ROWS, 1792), BF),
+            pltpu.VMEM((CHUNKS, 7, ROWS, 1792), BF),
+            pltpu.VMEM((CHUNKS, ROWS, 896), BF),
+            pltpu.VMEM((CHUNKS, CHIPS, 2, ROWS, 896), BF),
+            pltpu.VMEM((CHUNKS, 2, 8, ROWS, 512), BF),
+            pltpu.VMEM((CHUNKS, 7, 2, ROWS, 512), BF),
+            pltpu.VMEM((CHUNKS, ROWS, 512), BF),
+            pltpu.VMEM((CHUNKS, ROWS, 512), BF),
+            pltpu.VMEM((CHUNKS, ROWS, 512), F32),
+            pltpu.VMEM((CHUNKS, CHIPS, 2, ROWS, 512), BF),
+            pltpu.SemaphoreType.DMA((3,)),
+            pltpu.SemaphoreType.DMA((8, CHUNKS)),
+            pltpu.SemaphoreType.DMA((8, CHUNKS)),
+        ],
+        compiler_params=pltpu.CompilerParams(
+            collective_id=0, has_side_effects=True, vmem_limit_bytes=36 * 1024 * 1024
+        ),
+        name="ffn_block",
+    )(ffn_input.reshape(CHIPS, 2, 64, 512), w_gate_up, w_down, stream)
+
+
 def body(ffn_input, w_gate_up, w_down, stream, attn_gain, w_query, w_kv, cache_kv, cache_len):
-    ff_width = w_gate_up.shape[2]
-    token_count = ffn_input.shape[0]
-    row_block = ffn_input
-    product = jnp.einsum("td,edf->tef", row_block, w_gate_up, preferred_element_type=jnp.float32)
-    summed = lax.psum(product.reshape(token_count, 2 * ff_width), ("seq", "tensor"))
-    hidden = (jax.nn.silu(summed[:, :ff_width]) * summed[:, ff_width:]).astype(jnp.bfloat16)
     group_rows = stream.shape[0]
-    row_block = hidden
-    ffn_out = lax.psum_scatter(
-        jnp.dot(row_block, w_down, preferred_element_type=jnp.float32),
-        "pipe",
-        scatter_dimension=0,
-        tiled=True,
-    )
-    mixed = (stream.astype(jnp.float32) + ffn_out).astype(jnp.bfloat16)
-    full_rows = lax.all_gather(mixed, ("seq", "tensor"), axis=1, tiled=True)
+    mixed, full_rows = ffn_block(ffn_input, w_gate_up, w_down, stream)
     wide = full_rows.astype(jnp.float32)
     mean_sq = jnp.mean(wide * wide, axis=1, keepdims=True)
     normed = (wide * lax.rsqrt(mean_sq + norm_eps) * attn_gain).astype(jnp.bfloat16)

time: 425 us -> 87.5 us (0.21)
  waiting for transfers between devices: 386 us -> 0 us
  Pallas kernels: 0 us -> 75.4 us
  matrix products: 17.9 us -> 2.97 us
  between operations: 14.6 us -> 1.78 us
    reduce_scatter x1 -> x0, waiting for transfers between devices: 201 us -> none  [body(): lax.psum_scatter(jnp.dot(row_block, w_down, preferred_element_type=jnp.fl...]
    psum x1 -> x0, waiting for transfers between devices: 147 us -> none  [body(): lax.psum(product.reshape(token_count, 2 * ff_width), ('seq', 'tensor'))]
    pallas_call x0 -> x1, Pallas kernels: none -> 75.4 us  [ffn_block(): pl.pallas_call(ffn_kernel, out_shape=(jax.ShapeDtypeStruct((64, 512), BF)...]
    all_gather x1 -> x0, waiting for transfers between devices: 38.3 us -> none  [body(): full_rows = lax.all_gather(mixed, ('seq', 'tensor'), axis=1, tiled=True)]
    dot_general x2 -> x0, matrix products: 12.2 us -> none  [the longest x1 6.36 us: body(): jnp.einsum('td,edf->tef', row_block, w_gate_up, preferred_element_type=jn...]
  transfers between devices with their start and end apart: 3 -> 0, of which waited for: 3 -> 0; matrix products, arithmetic and copies ran while one was open for 0% -> 0% of each run, Pallas kernels for 0% -> 0%
where the time goes in v1:
time: 87.5 us; the launch traced here: 87.3 us
  Pallas kernels  75.4 us (86%)
  local copies, waits for them, and re-layouts  6.04 us (7%)
  matrix products  2.97 us (3%)
  between operations  1.78 us (2%)
  other arithmetic  1.1 us (1%)
    pallas_call x1, Pallas kernels, ffn_block(): pl.pallas_call(ffn_kernel, out_shape=(jax.ShapeDtypeStruct((64, 512), BF)...  75.4 us
    unnamed x18, local copies, waits for them, and re-layouts  6.03 us

profile of v1, /device:TPU:1, one launch (start us, length us, event | category | flops | bytes accessed | tf_op | source)
XLA Modules:
  0.0 87.3 jit_solution(3054492179465243099)
XLA Ops:
  0.6 0.0 copy-start
  0.6 1.5 %copy-done = bf16[2,512,896]{2,1,0:T(8,128)(2,1)S(1)} copy-done((bf16[2,512,896]{2,1,0:T(8,128)(2,1)S(1)}, bf16[2,512,896]{2,1,0:T(8,128)(2,1)}, u32[]{:S(2)}) %copy-start) | copy-done | bytes 1835032
  2.1 0.0 copy-start.1
  2.1 1.2 %copy-done.1 = bf16[1024,512]{1,0:T(8,128)(2,1)S(1)} copy-done((bf16[1024,512]{1,0:T(8,128)(2,1)S(1)}, bf16[1024,512]{1,0:T(8,128)(2,1)}, u32[]{:S(2)}) %copy-start.1) | copy-done | bytes 1048600
  3.4 0.0 copy-start.2
  3.4 1.2 %copy-done.2 = bf16[896,512]{1,0:T(8,128)(2,1)S(1)} copy-done((bf16[896,512]{1,0:T(8,128)(2,1)S(1)}, bf16[896,512]{1,0:T(8,128)(2,1)}, u32[]{:S(2)}) %copy-start.2) | copy-done | bytes 917528
  4.5 0.0 copy-start.3
  4.5 0.8 copy-done.3
  5.4 0.0 copy-start.5
  5.4 0.0 copy-start.7
  5.4 75.4 %ffn_block.1 = (bf16[64,512]{1,0:T(8,128)(2,1)S(1)}, bf16[64,8192]{1,0:T(8,128)(2,1)S(1)}) custom-call(bf16[8,2,64,512]{3,2,1,0:T(8,128)(2,1)S(1)} %bitcast.76, bf16[2,512,896]{2,1,0:T(8,128)(2,1)S(1)} %copy-done, bf16[896,512]{1,0:T(8,128)(2,1)S(1)} %copy-done.2, bf16[64,512]{1,0:T(8,128)(2,1)S(1)} %copy-done.3), custom_call_target="tpu_custom_call" | custom-call | tf_op jit(solution)/shard_map/ffn_block/pallas_call | solution.py:264
  80.8 0.3 fusion.4
  81.1 0.0 copy-done.5
  81.1 0.0 copy-done.7
  81.1 0.0 copy-start.6
  81.1 0.9 %fusion.10 = f32[64,1,2,128]{3,0,2,1:T(8,128)S(1)} fusion(bf16[8192,2,128]{2,1,0:T(2,128)(2,1)S(1)} %bitcast.77, bf16[64,8192]{1,0:T(8,128)(2,1)S(1)} %get-tuple-element.5, f32[8192]{0:T(1024)S(1)} %copy-done.7, f32[64]{0:T(128)S(1)} %add_rsqrt_fusion), kind=kOutput, calls=%fused_computation.13 | convolution fusion | flops 270532608 | bytes 5341440 | tf_op jit(solution)/shard_map/td,dkgh->tkgh/dot_general | solution.py:305
  83.1 0.2 multiply_cosine_fusion.1
  83.3 0.1 fusion.38
  83.4 0.0 copy-done.6
  83.4 0.0 copy-start.4
  83.4 0.9 %fusion.13 = f32[64,2,1,128]{3,0,1,2:T(8,128)S(1)} fusion(bf16[8192,2,128]{2,1,0:T(2,128)(2,1)S(1)} %bitcast.78, bf16[64,8192]{1,0:T(8,128)(2,1)S(1)} %get-tuple-element.5, f32[8192]{0:T(1024)S(1)} %copy-done.7, f32[64]{0:T(128)S(1)} %add_rsqrt_fusion), kind=kOutput, calls=%fused_computation.14 | convolution fusion | flops 270532608 | bytes 5341440 | tf_op jit(solution)/shard_map/td,dekh->tekh/dot_general | solution.py:306
  84.3 0.2 fusion.47
  84.5 0.3 fusion.51
  84.8 0.0 copy-done.4
  84.8 0.4 fusion.50
  85.2 0.2 fusion.23
  85.5 0.3 convolution_bitcast_fusion
  85.8 0.2 fusion.19
  86.0 0.6 copy.14
  86.7 0.6 copy.26
  (9 shorter events, 0.1 us)
Async XLA Ops:
  0.6 1.5 %copy-start = (bf16[2,512,896]{2,1,0:T(8,128)(2,1)S(1)}, bf16[2,512,896]{2,1,0:T(8,128)(2,1)}, u32[]{:S(2)}) copy-start(bf16[2,512,896]{2,1,0:T(8,128)(2,1)} %wgu_hbm.1) | copy-start | bytes 5505028
  2.1 1.2 %copy-start.1 = (bf16[1024,512]{1,0:T(8,128)(2,1)S(1)}, bf16[1024,512]{1,0:T(8,128)(2,1)}, u32[]{:S(2)}) copy-start(bf16[1024,512]{1,0:T(8,128)(2,1)} %param.9) | copy-start | bytes 3145732
  3.4 1.2 %copy-start.2 = (bf16[896,512]{1,0:T(8,128)(2,1)S(1)}, bf16[896,512]{1,0:T(8,128)(2,1)}, u32[]{:S(2)}) copy-start(bf16[896,512]{1,0:T(8,128)(2,1)} %wd_hbm.1) | copy-start | bytes 2752516
  4.5 0.8 copy-start.3
  5.4 75.7 %copy-start.5 = (bf16[8192,1,2,128]{3,2,1,0:T(2,128)(2,1)S(1)}, bf16[8192,1,2,128]{3,2,1,0:T(2,128)(2,1)}, u32[]{:S(2)}) copy-start(bf16[8192,1,2,128]{3,2,1,0:T(2,128)(2,1)} %param.14) | copy-start | bytes 12582916
  5.4 75.7 %copy-start.7 = (f32[8192]{0:T(1024)S(1)}, f32[8192]{0:T(1024)}, u32[]{:S(2)}) copy-start(f32[8192]{0:T(1024)} %param.13) | copy-start | bytes 98308
  81.1 2.2 %copy-start.6 = (bf16[8192,2,1,128]{3,1,2,0:T(2,128)(2,1)S(1)}, bf16[8192,2,1,128]{3,1,2,0:T(2,128)(2,1)}, u32[]{:S(2)}) copy-start(bf16[8192,2,1,128]{3,1,2,0:T(2,128)(2,1)} %param.15) | copy-start | bytes 12582916
  83.4 1.4 %copy-start.4 = (bf16[1,2,1024,1,128]{4,2,3,1,0:T(8,128)(2,1)S(1)}, bf16[1,2,1024,1,128]{4,2,3,1,0:T(8,128)(2,1)}, u32[]{:S(2)}) copy-start(bf16[1,2,1024,1,128]{4,2,3,1,0:T(8,128)(2,1)} %param.16) | copy-start | bytes 1572868

commit v2 on v1

v2 whole, which is shorter than its diff:
```python
import math

import jax
import jax.numpy as jnp
from jax import lax
from jax.experimental import pallas as pl
from jax.experimental.pallas import tpu as pltpu
from jax.sharding import PartitionSpec as P

norm_eps = 1e-05
rope_theta = 500000.0
MESH = pl.DeviceIdType.MESH
BF = jnp.bfloat16
F32 = jnp.float32

CHUNKS = 4
ROWS = 16
CHIPS = 8
OFFSETS = [(a, b) for a in range(2) for b in range(4)][1:]
WA, WB = 512, 384
KINDS = 19
(CORE, A1, B1, A2, B2, AY, AX, AR, BX, BY, BR, FA, FB, Z, ZH, ZF, XH, G, GF) = range(KINDS)
ORDER = (
    "a0", "a1", "b0", "a2", "b1", "r0", "a3", "b2", "c0", "b3", "w0",
    "c1", "j0", "w1", "c2", "j1", "w2", "d0", "c3", "j2", "w3", "d1",
    "k0", "j3", "e0", "w4", "d2", "k1", "e1", "w5", "d3", "k2", "q0",
    "e2", "w6", "k3", "q1", "e3", "w7", "g0", "q2", "g1", "q3", "h0",
    "g2", "i0", "h1", "g3", "i1", "h2", "i2", "h3", "i3", "t0",
)


def wait_bytes(ref, sem):
    pltpu.make_async_copy(ref, ref, sem).wait()


def ffn_kernel(
    x_hbm,
    wgu_hbm,
    wd_hbm,
    stream_ref,
    gain_ref,
    wq_hbm,
    wkv_hbm,
    cache_hbm,
    len_ref,
    mixed_ref,
    attended_ref,
    x_v,
    wgu_v,
    wd_v,
    core_send,
    core_recv,
    a_send,
    b_send,
    a_recv,
    b_recv,
    a_send2,
    a_recv2,
    b_own2,
    b_send2,
    b_recv2,
    hid_own,
    hid_a,
    hid_b,
    z_send,
    z_recv,
    zh_recv,
    zf_send,
    zf_recv,
    xh_recv,
    full_all,
    wq_v,
    wkv_v,
    cache_v,
    wide_w,
    spread,
    w_all,
    normed,
    cosine,
    sine,
    load_sem,
    send_sem,
    recv_sem,
):
    p = lax.axis_index("pipe")
    s = lax.axis_index("seq")
    t = lax.axis_index("tensor")
    xh, z = p // 8, p % 8
    y, core = t // 2, t % 2
    sibling = (p, s, y * 2 + 1 - core)
    seq_peer = (p, 1 - s, t)
    x_peer = ((1 - xh) * 8 + z, s, t)

    loads = [
        pltpu.make_async_copy(src, dst, load_sem.at[i])
        for i, (src, dst) in enumerate(
            (
                (x_hbm, x_v),
                (wgu_hbm, wgu_v),
                (wd_hbm, wd_v),
                (wq_hbm, wq_v),
                (wkv_hbm, wkv_v),
                (cache_hbm, cache_v),
            )
        )
    ]
    loads[0].start()
    loads[1].start()

    def y_peer(dy):
        y2 = (y + dy) % 4
        return y2, (p, s, y2 * 2 + core)

    def group_peer(da, dy):
        return (p, (s + da) % 2, (y + dy) % 4 * 2 + core)

    def z_peer(dz):
        z2 = (z + dz) % 8
        return z2, (xh * 8 + z2, s, t)

    def cross_peer(dz):
        return ((1 - xh) * 8 + (z + dz) % 8, s, t)

    barrier = pltpu.get_barrier_semaphore()
    everyone = [sibling, x_peer]
    everyone += [group_peer(*o) for o in OFFSETS]
    everyone += [z_peer(dz)[1] for dz in (1, 2, 3, 5, 6, 7)]
    everyone += [cross_peer(sign) for sign in (1, -1)]
    for peer in everyone:
        pl.semaphore_signal(barrier, inc=1, device_id=peer, device_id_type=MESH)

    def send(src, dst, kind, c, peer):
        pltpu.make_async_remote_copy(
            src_ref=src,
            dst_ref=dst,
            send_sem=send_sem.at[kind, c],
            recv_sem=recv_sem.at[kind, c],
            device_id=peer,
            device_id_type=MESH,
        ).start()

    def arrivals(kind, c):
        return {
            CORE: core_recv.at[c],
            A1: a_recv.at[c],
            B1: b_recv.at[c],
            A2: a_recv2.at[c],
            B2: b_recv2.at[c],
            AY: hid_a.at[c, 0, 0:3, 0],
            AX: hid_a.at[c, 0, 0, 0],
            AR: hid_a.at[c, 0, 0:3, 0],
            BX: hid_b.at[c, 0, 0, 0],
            BY: hid_b.at[c, 0, 0:3, 0],
            BR: hid_b.at[c, 0, 0:3, 0],
            FA: hid_a.at[c, :, :, 0],
            FB: hid_b.at[c, :, :, 0],
            Z: z_recv.at[c],
            ZH: zh_recv.at[c],
            ZF: zf_recv.at[c],
            XH: xh_recv.at[c],
            G: full_all.at[c, 0:7, 0],
            GF: full_all.at[c, :, 0],
        }[kind]

    def arrived(kind, c):
        wait_bytes(arrivals(kind, c), recv_sem.at[kind, c])

    def sent(kind, c):
        wait_bytes(arrivals(kind, c), send_sem.at[kind, c])

    def gate_up(rows, c):
        left = x_v[:, rows, pl.ds(c * ROWS, ROWS), :].reshape(CHIPS * ROWS, 512)
        return [
            jnp.dot(left, wgu_v[e], preferred_element_type=F32).reshape(CHIPS, ROWS, 896)
            for e in range(2)
        ]

    def stage_a(c):
        for e, part in enumerate(gate_up(1 - core, c)):
            core_send[c, :, :, e * 896 : (e + 1) * 896] = part.astype(BF)
        send(core_send.at[c], core_recv.at[c], CORE, c, sibling)

    def stage_b(c):
        parts = gate_up(core, c)
        arrived(CORE, c)
        for e, part in enumerate(parts):
            total = part + core_recv[c, :, :, e * 896 : (e + 1) * 896].astype(F32)
            total = total.astype(BF).reshape(2, 4, ROWS, 896)
            a_send[c, :, :, :, e * WA : (e + 1) * WA] = total[..., :WA]
            b_send[c, :, :, :, e * WB : (e + 1) * WB] = total[..., WA:]
        send(a_send.at[c, 1 - s], a_recv.at[c], A1, c, seq_peer)
        for dy in range(1, 4):
            y2, peer = y_peer(dy)
            send(b_send.at[c, :, y2], b_recv.at[c, dy - 1], B1, c, peer)

    def stage_c(c):
        arrived(A1, c)
        a_send2[c] = (a_send[c, s].astype(F32) + a_recv[c].astype(F32)).astype(BF)
        for dy in range(1, 4):
            y2, peer = y_peer(dy)
            send(a_send2.at[c, y2], a_recv2.at[c, dy - 1], A2, c, peer)
        arrived(B1, c)

        def total(a):
            value = b_send[c, a, y].astype(F32)
            for j in range(3):
                value = value + b_recv[c, j, a].astype(F32)
            return value

        b_send2[c] = total(1 - s).astype(BF)
        send(b_send2.at[c], b_recv2.at[c], B2, c, seq_peer)
        b_own2[c] = total(s)

    def stage_j(c):
        def swiglu(total, width):
            return (jax.nn.silu(total[:, :width]) * total[:, width:]).astype(BF)

        arrived(A2, c)
        total = a_send2[c, y].astype(F32)
        for j in range(3):
            total = total + a_recv2[c, j].astype(F32)
        hidden = swiglu(total, WA)
        hid_own[c, :, :WA] = hidden
        hid_a[c, s, y, core] = hidden
        own = hid_own.at[c, :, 0:WA]
        for dy in range(1, 4):
            send(own, hid_a.at[c, s, y, core], AY, c, y_peer(dy)[1])
        send(own, hid_a.at[c, s, y, core], AX, c, seq_peer)
        arrived(B2, c)
        hidden = swiglu(b_own2[c] + b_recv2[c].astype(F32), WB)
        hid_own[c, :, WA:] = hidden
        hid_b[c, s, y, core] = hidden
        own = hid_own.at[c, :, WA : WA + WB]
        send(own, hid_b.at[c, s, y, core], BX, c, seq_peer)
        for dy in range(1, 4):
            send(own, hid_b.at[c, s, y, core], BY, c, y_peer(dy)[1])

    def stage_d(c):
        arrived(AY, c)
        for dy in range(1, 4):
            y2, _ = y_peer(dy)
            send(hid_a.at[c, s, y2, core], hid_a.at[c, s, y2, core], AR, c, seq_peer)
        arrived(BX, c)
        for dy in range(1, 4):
            block = hid_b.at[c, 1 - s, y, core]
            send(block, block, BR, c, y_peer(dy)[1])

    def stage_k(c):
        arrived(AX, c)
        arrived(AR, c)
        send(hid_a.at[c, :, :, core], hid_a.at[c, :, :, core], FA, c, sibling)
        arrived(BY, c)
        arrived(BR, c)
        send(hid_b.at[c, :, :, core], hid_b.at[c, :, :, core], FB, c, sibling)

    def stage_e(c):
        arrived(FA, c)
        arrived(FB, c)
        out = jnp.dot(
            hid_a[c].reshape(256, WA), wd_v[:WA, :], preferred_element_type=F32
        ) + jnp.dot(hid_b[c].reshape(256, WB), wd_v[WA:, :], preferred_element_type=F32)
        z_send[c] = out.astype(BF).reshape(2, 8, ROWS, 512)
        send(z_send.at[c, 1 - xh, z], xh_recv.at[c], XH, c, x_peer)
        for way, sign in enumerate((1, -1)):
            for hop in (1, 2):
                z2, _ = z_peer(sign * (hop + 1))
                _, peer = z_peer(sign * hop)
                send(z_send.at[c, :, z2], z_recv.at[c, way, hop - 1], Z, c, peer)
            z2, _ = z_peer(4)
            _, peer = z_peer(sign * 3)
            half = pl.ds(way * 256, 256)
            send(z_send.at[c, :, z2, :, half], zh_recv.at[c, way], ZH, c, peer)

    def stage_q(c):
        arrived(Z, c)
        arrived(ZH, c)
        for way, sign in enumerate((1, -1)):
            z2, peer = z_peer(sign)
            for h in range(2):
                cols = slice(h * 256, (h + 1) * 256)
                total = z_send[c, :, z2, :, cols].astype(F32)
                for hop in range(2):
                    total = total + z_recv[c, way, hop, :, :, cols].astype(F32)
                if h == way:
                    total = total + zh_recv[c, way].astype(F32)
                zf_send[c, way, :, :, cols] = total.astype(BF)
            send(zf_send.at[c, way, xh], zf_recv.at[c, way, 0], ZF, c, peer)
            send(zf_send.at[c, way, 1 - xh], zf_recv.at[c, way, 1], ZF, c, cross_peer(sign))

    def stage_g(c):
        arrived(XH, c)
        arrived(ZF, c)
        rows = slice(c * ROWS, (c + 1) * ROWS)
        ffn_out = z_send[c, xh, z].astype(F32) + xh_recv[c].astype(F32)
        for way in range(2):
            for side in range(2):
                ffn_out = ffn_out + zf_recv[c, way, side].astype(F32)
        mixed = (stream_ref[rows, :].astype(F32) + ffn_out).astype(BF)
        mixed_ref[rows, :] = mixed
        full_all[c, s * 4 + y, core] = mixed
        for o in OFFSETS:
            send(mixed_ref.at[rows], full_all.at[c, s * 4 + y, core], G, c, group_peer(*o))

    def stage_h(c):
        arrived(G, c)
        send(full_all.at[c, :, core], full_all.at[c, :, core], GF, c, sibling)

    def stage_i(c):
        arrived(GF, c)
        rows = slice(c * ROWS, (c + 1) * ROWS)
        squares = jnp.zeros((ROWS, 1), F32)
        for m in range(16):
            wide = full_all[c, m // 2, m % 2].astype(F32)
            squares = squares + jnp.sum(wide * wide, axis=1, keepdims=True)
        scale = lax.rsqrt(squares * (1.0 / 8192) + norm_eps)
        for m in range(16):
            cols = slice(m * 512, (m + 1) * 512)
            wide = full_all[c, m // 2, m % 2].astype(F32)
            normed[rows, cols] = (wide * scale * gain_ref[:, cols]).astype(BF)

    def stage_w(n):
        if n == 0:
            loads[3].wait()
            loads[4].wait()
        for which, source in enumerate((wq_v, wkv_v)):
            for part in range(2):
                at = n * 1024 + part * 512
                wide_w[...] = source[2 * at : 2 * at + 1024, :].astype(F32)
                for e in range(2):
                    cols = slice((2 * which + e) * 128, (2 * which + e + 1) * 128)
                    w_all[at : at + 512, cols] = wide_w[pl.ds(e, 512, stride=2), :].astype(BF)

    def stage_r(_):
        lane = lax.broadcasted_iota(jnp.int32, (64, 128), 1)
        half = lax.rem(lane, 64)
        inv_freq = jnp.exp(half.astype(F32) * (-2.0 * math.log(rope_theta) / 128))
        row = lax.broadcasted_iota(jnp.int32, (64, 128), 0)
        angles = (len_ref[0] + row).astype(F32) * inv_freq
        cosine[...] = jnp.cos(angles)
        sine[...] = jnp.where(lane < 64, -1.0, 1.0) * jnp.sin(angles)

    def stage_t(_):
        def step(i, total):
            cols = pl.ds(pl.multiple_of(i * 1024, 1024), 1024)
            return total + jnp.dot(
                normed[:, cols], w_all[cols, :], preferred_element_type=F32
            )

        total = lax.fori_loop(0, 8, step, jnp.zeros((64, 512), F32))

        def rotated(value):
            return (value * cosine[...] + pltpu.roll(value, 64, 1) * sine[...]).astype(BF)

        queries = jnp.concatenate([rotated(total[:, :128]), rotated(total[:, 128:256])], axis=0)
        k_new = rotated(total[:, 256:384])
        v_new = total[:, 384:].astype(BF)
        loads[5].wait()
        head_scale = 128 ** (-0.5)
        dims = (((1,), (1,)), ((), ()))
        cache_scores = (
            lax.dot_general(queries, cache_v[0], dims, preferred_element_type=F32) * head_scale
        )
        own_scores = lax.dot_general(queries, k_new, dims, preferred_element_type=F32) * head_scale
        spot = lax.broadcasted_iota(jnp.int32, (128, 1024), 1)
        cache_scores = jnp.where(spot < len_ref[0], cache_scores, -1e30)
        row = lax.rem(lax.broadcasted_iota(jnp.int32, (128, 64), 0), 64)
        spot = lax.broadcasted_iota(jnp.int32, (128, 64), 1)
        own_scores = jnp.where(spot <= row, own_scores, -1e30)
        row_max = jnp.maximum(
            jnp.max(cache_scores, axis=1, keepdims=True), jnp.max(own_scores, axis=1, keepdims=True)
        )
        cache_exp = jnp.exp(cache_scores - row_max)
        own_exp = jnp.exp(own_scores - row_max)
        denominator = jnp.sum(cache_exp, axis=1, keepdims=True) + jnp.sum(
            own_exp, axis=1, keepdims=True
        )
        cache_w = (cache_exp / denominator).astype(BF)
        own_w = (own_exp / denominator).astype(BF)
        result = jnp.dot(cache_w, cache_v[1], preferred_element_type=F32)
        result = result + jnp.dot(own_w, v_new, preferred_element_type=F32)
        for g in range(2):
            spread[pl.ds(g, 64, stride=2), :] = result[g * 64 : (g + 1) * 64]
        attended_ref[...] = spread[...].astype(BF)

    loads[0].wait()
    loads[1].wait()
    for load in loads[2:]:
        load.start()
    pl.semaphore_wait(barrier, len(everyone))
    stages = dict(
        a=stage_a,
        b=stage_b,
        c=stage_c,
        j=stage_j,
        d=stage_d,
        k=stage_k,
        e=stage_e,
        q=stage_q,
        g=stage_g,
        h=stage_h,
        i=stage_i,
        w=stage_w,
        r=stage_r,
        t=stage_t,
    )
    waited = False
    for step in ORDER:
        if step[0] == "e" and not waited:
            loads[2].wait()
            waited = True
        stages[step[0]](int(step[1]))

    for c in range(CHUNKS):
        for kind in range(KINDS):
            sent(kind, c)


def ffn_block(ffn_input, w_gate_up, w_down, stream, attn_gain, w_query, w_kv, cache_kv, cache_len):
    vmem = pl.BlockSpec(memory_space=pltpu.VMEM)
    hbm = pl.BlockSpec(memory_space=pl.ANY)
    smem = pl.BlockSpec(memory_space=pltpu.SMEM)
    mixed, attended = pl.pallas_call(
        ffn_kernel,
        out_shape=(
            jax.ShapeDtypeStruct((64, 512), BF),
            jax.ShapeDtypeStruct((128, 128), BF),
        ),
        in_specs=[hbm, hbm, hbm, vmem, vmem, hbm, hbm, hbm, smem],
        out_specs=(vmem, vmem),
        scratch_shapes=[
            pltpu.VMEM((CHIPS, 2, 64, 512), BF),
            pltpu.VMEM((2, 512, 896), BF),
            pltpu.VMEM((896, 512), BF),
            pltpu.VMEM((CHUNKS, CHIPS, ROWS, 1792), BF),
            pltpu.VMEM((CHUNKS, CHIPS, ROWS, 1792), BF),
            pltpu.VMEM((CHUNKS, 2, 4, ROWS, 2 * WA), BF),
            pltpu.VMEM((CHUNKS, 2, 4, ROWS, 2 * WB), BF),
            pltpu.VMEM((CHUNKS, 4, ROWS, 2 * WA), BF),
            pltpu.VMEM((CHUNKS, 3, 2, ROWS, 2 * WB), BF),
            pltpu.VMEM((CHUNKS, 4, ROWS, 2 * WA), BF),
            pltpu.VMEM((CHUNKS, 3, ROWS, 2 * WA), BF),
            pltpu.VMEM((CHUNKS, ROWS, 2 * WB), F32),
            pltpu.VMEM((CHUNKS, ROWS, 2 * WB), BF),
            pltpu.VMEM((CHUNKS, ROWS, 2 * WB), BF),
            pltpu.VMEM((CHUNKS, ROWS, 896), BF),
            pltpu.VMEM((CHUNKS, 2, 4, 2, ROWS, WA), BF),
            pltpu.VMEM((CHUNKS, 2, 4, 2, ROWS, WB), BF),
            pltpu.VMEM((CHUNKS, 2, 8, ROWS, 512), BF),
            pltpu.VMEM((CHUNKS, 2, 2, 2, ROWS, 512), BF),
            pltpu.VMEM((CHUNKS, 2, 2, ROWS, 256), BF),
            pltpu.VMEM((CHUNKS, 2, 2, ROWS, 512), BF),
            pltpu.VMEM((CHUNKS, 2, 2, ROWS, 512), BF),
            pltpu.VMEM((CHUNKS, ROWS, 512), BF),
            pltpu.VMEM((CHUNKS, CHIPS, 2, ROWS, 512), BF),
            pltpu.VMEM((16384, 128), BF),
            pltpu.VMEM((16384, 128), BF),
            pltpu.VMEM((2, 1024, 128), BF),
            pltpu.VMEM((1024, 128), F32),
            pltpu.VMEM((128, 128), F32),
            pltpu.VMEM((8192, 512), BF),
            pltpu.VMEM((64, 8192), BF),
            pltpu.VMEM((64, 128), F32),
            pltpu.VMEM((64, 128), F32),
            pltpu.SemaphoreType.DMA((6,)),
            pltpu.SemaphoreType.DMA((KINDS, CHUNKS)),
            pltpu.SemaphoreType.DMA((KINDS, CHUNKS)),
        ],
        compiler_params=pltpu.CompilerParams(
            collective_id=0, has_side_effects=True, vmem_limit_bytes=58 * 1024 * 1024
        ),
        name="ffn_block",
    )(
        ffn_input.reshape(CHIPS, 2, 64, 512),
        w_gate_up,
        w_down,
        stream,
        attn_gain.reshape(1, 8192),
        w_query.reshape(16384, 128),
        w_kv.reshape(16384, 128),
        cache_kv.reshape(2, 1024, 128),
        cache_len,
    )
    return mixed, attended.reshape(64, 1, 2, 128)


def solution(mesh):
    in_specs = (
        P(None, ("seq", "tensor")),
        P(None, ("seq", "tensor"), "pipe"),
        P("pipe", ("seq", "tensor")),
        P("pipe", ("seq", "tensor")),
        P(),
        P(None, "tensor", "seq", None),
        P(None, None, "tensor", None),
        P("pipe", None, None, "tensor", None),
        P("pipe"),
    )
    out_specs = (P("pipe", ("seq", "tensor")), P("pipe", "tensor", "seq", None))
    return jax.shard_map(ffn_block, mesh=mesh, in_specs=in_specs, out_specs=out_specs, check_vma=False)
```

time: 87.5 us -> 71.7 us (0.82)
  Pallas kernels: 75.4 us -> 67.2 us
  local copies, waits for them, and re-layouts: 6.04 us -> 2.87 us
  matrix products: 2.97 us -> 0 us
  other arithmetic: 1.1 us -> 0 us
    pallas_call x1, Pallas kernels: 75.4 us -> 67.2 us  [ffn_block(): pl.pallas_call(ffn_kernel, out_shape=(jax.ShapeDtypeStruct((64, 512), BF)...]
    unnamed x18 -> x2, local copies, waits for them, and re-layouts: 6.03 us -> 2.87 us
    dot_general x6 -> x0, matrix products: 2.97 us -> none  [the longest x1 0.92 us: body(): jnp.einsum('td,dekh->tekh', normed, w_kv, preferred_element_type=jnp.floa...]
where the time goes in v2:
time: 71.7 us; the launch traced here: 71.4 us
  Pallas kernels  67.2 us (94%)
  local copies, waits for them, and re-layouts  2.87 us (4%)
  between operations  1.29 us (2%)
    pallas_call x1, Pallas kernels, ffn_block(): pl.pallas_call(ffn_kernel, out_shape=(jax.ShapeDtypeStruct((64, 512), BF)...  67.2 us
    unnamed x2, local copies, waits for them, and re-layouts  2.87 us

profile of v2, /device:TPU:1, one launch (start us, length us, event | category | flops | bytes accessed | tf_op | source)
XLA Modules:
  0.0 71.4 jit_solution(1579995328251265045)
XLA Ops:
  1.3 67.2 %ffn_block.1 = (bf16[64,512]{1,0:T(8,128)(2,1)}, bf16[128,128]{1,0:T(8,128)(2,1)}) custom-call(bf16[8,2,64,512]{3,2,1,0:T(8,128)(2,1)} %bitcast.10, bf16[2,512,896]{2,1,0:T(8,128)(2,1)} %wgu_hbm.1, bf16[896,512]{1,0:T(8,128)(2,1)} %wd_hbm.1, bf16[64,512]{1,0:T(8,128)(2,1)} %stream_ref.1, f32[1,8192]{1,0:T(1,128)} %bitcast.12, bf16[16384,128]{1,0:T(8,128)(2,1)} %bitcast.8, ...), custom_call_target="tpu_custom_call" | custom-call | tf_op jit(solution)/shard_map/ffn_block/pallas_call | solution.py:422
  68.5 1.5 %copy.15 = bf16[64,512]{1,0:T(8,128)(2,1)} copy(bf16[64,512]{1,0:T(8,128)(2,1)} %get-tuple-element.10) | data formatting | bytes 131072
  70.0 1.4 %copy.16 = bf16[64,1,2,128]{3,2,1,0:T(2,128)(2,1)} copy(bf16[64,1,2,128]{3,2,1,0:T(2,128)(2,1)} %bitcast.13) | data formatting | bytes 65536

commit v3 on v2

--- a/solution.py
+++ b/solution.py
@@ -18,14 +18,14 @@
 CHIPS = 8
 OFFSETS = [(a, b) for a in range(2) for b in range(4)][1:]
 WA, WB = 512, 384
-KINDS = 19
-(CORE, A1, B1, A2, B2, AY, AX, AR, BX, BY, BR, FA, FB, Z, ZH, ZF, XH, G, GF) = range(KINDS)
+KINDS = 13
+(CORE, A1, B1, A2, B2, AG, AF, Z, ZH, ZF, XH, G, GF) = range(KINDS)
 ORDER = (
     "a0", "a1", "b0", "a2", "b1", "r0", "a3", "b2", "c0", "b3", "w0",
-    "c1", "j0", "w1", "c2", "j1", "w2", "d0", "c3", "j2", "w3", "d1",
-    "k0", "j3", "e0", "w4", "d2", "k1", "e1", "w5", "d3", "k2", "q0",
-    "e2", "w6", "k3", "q1", "e3", "w7", "g0", "q2", "g1", "q3", "h0",
-    "g2", "i0", "h1", "g3", "i1", "h2", "i2", "h3", "i3", "t0",
+    "c1", "j0", "w1", "c2", "j1", "w2", "k0", "c3", "j2", "w3", "e0",
+    "k1", "j3", "w4", "e1", "k2", "q0", "w5", "e2", "k3", "q1", "w6",
+    "e3", "g0", "q2", "w7", "g1", "q3", "h0", "g2", "i0", "h1", "g3",
+    "i1", "h2", "i2", "h3", "i3", "t0",
 )
 
 
@@ -60,8 +60,7 @@
     b_send2,
     b_recv2,
     hid_own,
-    hid_a,
-    hid_b,
+    hid_all,
     z_send,
     z_recv,
     zh_recv,
@@ -146,14 +145,8 @@
             B1: b_recv.at[c],
             A2: a_recv2.at[c],
             B2: b_recv2.at[c],
-            AY: hid_a.at[c, 0, 0:3, 0],
-            AX: hid_a.at[c, 0, 0, 0],
-            AR: hid_a.at[c, 0, 0:3, 0],
-            BX: hid_b.at[c, 0, 0, 0],
-            BY: hid_b.at[c, 0, 0:3, 0],
-            BR: hid_b.at[c, 0, 0:3, 0],
-            FA: hid_a.at[c, :, :, 0],
-            FB: hid_b.at[c, :, :, 0],
+            AG: hid_all.at[c, 0:7, 0],
+            AF: hid_all.at[c, :, 0],
             Z: z_recv.at[c],
             ZH: zh_recv.at[c],
             ZF: zf_recv.at[c],
@@ -221,44 +214,20 @@
             total = total + a_recv2[c, j].astype(F32)
         hidden = swiglu(total, WA)
         hid_own[c, :, :WA] = hidden
-        hid_a[c, s, y, core] = hidden
-        own = hid_own.at[c, :, 0:WA]
-        for dy in range(1, 4):
-            send(own, hid_a.at[c, s, y, core], AY, c, y_peer(dy)[1])
-        send(own, hid_a.at[c, s, y, core], AX, c, seq_peer)
         arrived(B2, c)
-        hidden = swiglu(b_own2[c] + b_recv2[c].astype(F32), WB)
-        hid_own[c, :, WA:] = hidden
-        hid_b[c, s, y, core] = hidden
-        own = hid_own.at[c, :, WA : WA + WB]
-        send(own, hid_b.at[c, s, y, core], BX, c, seq_peer)
-        for dy in range(1, 4):
-            send(own, hid_b.at[c, s, y, core], BY, c, y_peer(dy)[1])
-
-    def stage_d(c):
-        arrived(AY, c)
-        for dy in range(1, 4):
-            y2, _ = y_peer(dy)
-            send(hid_a.at[c, s, y2, core], hid_a.at[c, s, y2, core], AR, c, seq_peer)
-        arrived(BX, c)
-        for dy in range(1, 4):
-            block = hid_b.at[c, 1 - s, y, core]
-            send(block, block, BR, c, y_peer(dy)[1])
+        hid_own[c, :, WA:] = swiglu(b_own2[c] + b_recv2[c].astype(F32), WB)
+        k = s * 4 + y
+        hid_all[c, k, core] = hid_own[c]
+        for o in OFFSETS:
+            send(hid_own.at[c], hid_all.at[c, k, core], AG, c, group_peer(*o))
 
     def stage_k(c):
-        arrived(AX, c)
-        arrived(AR, c)
-        send(hid_a.at[c, :, :, core], hid_a.at[c, :, :, core], FA, c, sibling)
-        arrived(BY, c)
-        arrived(BR, c)
-        send(hid_b.at[c, :, :, core], hid_b.at[c, :, :, core], FB, c, sibling)
+        arrived(AG, c)
+        send(hid_all.at[c, :, core], hid_all.at[c, :, core], AF, c, sibling)
 
     def stage_e(c):
-        arrived(FA, c)
-        arrived(FB, c)
-        out = jnp.dot(
-            hid_a[c].reshape(256, WA), wd_v[:WA, :], preferred_element_type=F32
-        ) + jnp.dot(hid_b[c].reshape(256, WB), wd_v[WA:, :], preferred_element_type=F32)
+        arrived(AF, c)
+        out = jnp.dot(hid_all[c].reshape(256, 896), wd_v[...], preferred_element_type=F32)
         z_send[c] = out.astype(BF).reshape(2, 8, ROWS, 512)
         send(z_send.at[c, 1 - xh, z], xh_recv.at[c], XH, c, x_peer)
         for way, sign in enumerate((1, -1)):
@@ -392,7 +361,6 @@
         b=stage_b,
         c=stage_c,
         j=stage_j,
-        d=stage_d,
         k=stage_k,
         e=stage_e,
         q=stage_q,
@@ -413,6 +381,11 @@
     for c in range(CHUNKS):
         for kind in range(KINDS):
             sent(kind, c)
+
+
+def hand_over(mixed_in, attended_in, mixed_out, attended_out):
+    mixed_out[...] = mixed_in[...]
+    attended_out[...] = attended_in[...]
 
 
 def ffn_block(ffn_input, w_gate_up, w_down, stream, attn_gain, w_query, w_kv, cache_kv, cache_len):
@@ -443,8 +416,7 @@
             pltpu.VMEM((CHUNKS, ROWS, 2 * WB), BF),
             pltpu.VMEM((CHUNKS, ROWS, 2 * WB), BF),
             pltpu.VMEM((CHUNKS, ROWS, 896), BF),
-            pltpu.VMEM((CHUNKS, 2, 4, 2, ROWS, WA), BF),
-            pltpu.VMEM((CHUNKS, 2, 4, 2, ROWS, WB), BF),
+            pltpu.VMEM((CHUNKS, CHIPS, 2, ROWS, 896), BF),
             pltpu.VMEM((CHUNKS, 2, 8, ROWS, 512), BF),
             pltpu.VMEM((CHUNKS, 2, 2, 2, ROWS, 512), BF),
             pltpu.VMEM((CHUNKS, 2, 2, ROWS, 256), BF),
@@ -480,6 +452,16 @@
         cache_kv.reshape(2, 1024, 128),
         cache_len,
     )
+    mixed, attended = pl.pallas_call(
+        hand_over,
+        out_shape=(
+            jax.ShapeDtypeStruct((64, 512), BF),
+            jax.ShapeDtypeStruct((128, 128), BF),
+        ),
+        in_specs=[vmem, vmem],
+        out_specs=(vmem, vmem),
+        name="hand_over",
+    )(mixed, attended)
     return mixed, attended.reshape(64, 1, 2, 128)
 
 

time: 71.7 us -> 68.5 us (0.955)
  local copies, waits for them, and re-layouts: 2.87 us -> 0 us
    unnamed x2 -> x0, local copies, waits for them, and re-layouts: 2.87 us -> none
    pallas_call x1, Pallas kernels: 67.2 us -> 65.6 us  [ffn_block(): pl.pallas_call(ffn_kernel, out_shape=(jax.ShapeDtypeStruct((64, 512), BF)...]
    pallas_call x0 -> x1, Pallas kernels: none -> 1.48 us  [ffn_block(): pl.pallas_call(hand_over, out_shape=(jax.ShapeDtypeStruct((64, 512), BF),...]
where the time goes in v3:
time: 68.5 us; the launch traced here: 68.3 us
  Pallas kernels  67 us (98%)
  between operations  1.29 us (2%)
    pallas_call x1, Pallas kernels, ffn_block(): pl.pallas_call(ffn_kernel, out_shape=(jax.ShapeDtypeStruct((64, 512), BF)...  65.6 us
    pallas_call x1, Pallas kernels, ffn_block(): pl.pallas_call(hand_over, out_shape=(jax.ShapeDtypeStruct((64, 512), BF),...  1.48 us

profile of v3, /device:TPU:1, one launch (start us, length us, event | category | flops | bytes accessed | tf_op | source)
XLA Modules:
  0.0 68.3 jit_solution(9030406336699337967)
XLA Ops:
  1.3 65.6 %ffn_block.1 = (bf16[64,512]{1,0:T(8,128)(2,1)}, bf16[128,128]{1,0:T(8,128)(2,1)}) custom-call(bf16[8,2,64,512]{3,2,1,0:T(8,128)(2,1)} %bitcast.10, bf16[2,512,896]{2,1,0:T(8,128)(2,1)} %wgu_hbm.1, bf16[896,512]{1,0:T(8,128)(2,1)} %wd_hbm.1, bf16[64,512]{1,0:T(8,128)(2,1)} %stream_ref.1, f32[1,8192]{1,0:T(1,128)} %bitcast.12, bf16[16384,128]{1,0:T(8,128)(2,1)} %bitcast.8, ...), custom_call_target="tpu_custom_call" | custom-call | tf_op jit(solution)/shard_map/ffn_block/pallas_call | solution.py:395
  66.8 1.5 %hand_over.1 = (bf16[64,512]{1,0:T(8,128)(2,1)}, bf16[128,128]{1,0:T(8,128)(2,1)}) custom-call(bf16[64,512]{1,0:T(8,128)(2,1)} %get-tuple-element.6.mixed_in, bf16[128,128]{1,0:T(8,128)(2,1)} %get-tuple-element.7.attended_in), custom_call_target="tpu_custom_call" | custom-call | tf_op jit(solution)/shard_map/hand_over/pallas_call | solution.py:455

commit v4 on v3

--- a/solution.py
+++ b/solution.py
@@ -16,7 +16,7 @@
 CHUNKS = 4
 ROWS = 16
 CHIPS = 8
-OFFSETS = [(a, b) for a in range(2) for b in range(4)][1:]
+OFFSETS = ((1, 2), (0, 2), (1, 1), (1, 3), (0, 1), (0, 3), (1, 0))
 WA, WB = 512, 384
 KINDS = 13
 (CORE, A1, B1, A2, B2, AG, AF, Z, ZH, ZF, XH, G, GF) = range(KINDS)
@@ -25,7 +25,7 @@
     "c1", "j0", "w1", "c2", "j1", "w2", "k0", "c3", "j2", "w3", "e0",
     "k1", "j3", "w4", "e1", "k2", "q0", "w5", "e2", "k3", "q1", "w6",
     "e3", "g0", "q2", "w7", "g1", "q3", "h0", "g2", "i0", "h1", "g3",
-    "i1", "h2", "i2", "h3", "i3", "t0",
+    "i1", "h2", "i2", "s0", "h3", "u0", "i3", "t0", "s1",
 )
 
 
@@ -77,6 +77,8 @@
     normed,
     cosine,
     sine,
+    scales,
+    projected,
     load_sem,
     send_sem,
     recv_sem,
@@ -171,6 +173,8 @@
     def stage_a(c):
         for e, part in enumerate(gate_up(1 - core, c)):
             core_send[c, :, :, e * 896 : (e + 1) * 896] = part.astype(BF)
+        if c == 0:
+            pl.semaphore_wait(barrier, len(everyone))
         send(core_send.at[c], core_recv.at[c], CORE, c, sibling)
 
     def stage_b(c):
@@ -182,14 +186,14 @@
             a_send[c, :, :, :, e * WA : (e + 1) * WA] = total[..., :WA]
             b_send[c, :, :, :, e * WB : (e + 1) * WB] = total[..., WA:]
         send(a_send.at[c, 1 - s], a_recv.at[c], A1, c, seq_peer)
-        for dy in range(1, 4):
+        for dy in (2, 1, 3):
             y2, peer = y_peer(dy)
             send(b_send.at[c, :, y2], b_recv.at[c, dy - 1], B1, c, peer)
 
     def stage_c(c):
         arrived(A1, c)
         a_send2[c] = (a_send[c, s].astype(F32) + a_recv[c].astype(F32)).astype(BF)
-        for dy in range(1, 4):
+        for dy in (2, 1, 3):
             y2, peer = y_peer(dy)
             send(a_send2.at[c, y2], a_recv2.at[c, dy - 1], A2, c, peer)
         arrived(B1, c)
@@ -229,16 +233,16 @@
         arrived(AF, c)
         out = jnp.dot(hid_all[c].reshape(256, 896), wd_v[...], preferred_element_type=F32)
         z_send[c] = out.astype(BF).reshape(2, 8, ROWS, 512)
-        send(z_send.at[c, 1 - xh, z], xh_recv.at[c], XH, c, x_peer)
         for way, sign in enumerate((1, -1)):
-            for hop in (1, 2):
+            z2, _ = z_peer(4)
+            half = pl.ds(way * 256, 256)
+            send(z_send.at[c, :, z2, :, half], zh_recv.at[c, way], ZH, c, z_peer(sign * 3)[1])
+        for hop in (2, 1):
+            for way, sign in enumerate((1, -1)):
                 z2, _ = z_peer(sign * (hop + 1))
                 _, peer = z_peer(sign * hop)
                 send(z_send.at[c, :, z2], z_recv.at[c, way, hop - 1], Z, c, peer)
-            z2, _ = z_peer(4)
-            _, peer = z_peer(sign * 3)
-            half = pl.ds(way * 256, 256)
-            send(z_send.at[c, :, z2, :, half], zh_recv.at[c, way], ZH, c, peer)
+        send(z_send.at[c, 1 - xh, z], xh_recv.at[c], XH, c, x_peer)
 
     def stage_q(c):
         arrived(Z, c)
@@ -270,22 +274,27 @@
         for o in OFFSETS:
             send(mixed_ref.at[rows], full_all.at[c, s * 4 + y, core], G, c, group_peer(*o))
 
+    def gained(c, which):
+        rows = slice(c * ROWS, (c + 1) * ROWS)
+        squares = jnp.zeros((ROWS, 1), F32)
+        for k in range(CHIPS):
+            wide = full_all[c, k, which].astype(F32)
+            gain = gain_ref[:, pl.ds(pl.multiple_of((k * 2 + which) * 512, 512), 512)]
+            squares = squares + jnp.sum(wide * wide, axis=1, keepdims=True)
+            normed[which, rows, k * 512 : (k + 1) * 512] = (wide * gain).astype(BF)
+        return squares
+
     def stage_h(c):
         arrived(G, c)
         send(full_all.at[c, :, core], full_all.at[c, :, core], GF, c, sibling)
+        rows = slice(c * ROWS, (c + 1) * ROWS)
+        scales[rows, :] = jnp.broadcast_to(gained(c, core), (ROWS, 128))
 
     def stage_i(c):
         arrived(GF, c)
         rows = slice(c * ROWS, (c + 1) * ROWS)
-        squares = jnp.zeros((ROWS, 1), F32)
-        for m in range(16):
-            wide = full_all[c, m // 2, m % 2].astype(F32)
-            squares = squares + jnp.sum(wide * wide, axis=1, keepdims=True)
-        scale = lax.rsqrt(squares * (1.0 / 8192) + norm_eps)
-        for m in range(16):
-            cols = slice(m * 512, (m + 1) * 512)
-            wide = full_all[c, m // 2, m % 2].astype(F32)
-            normed[rows, cols] = (wide * scale * gain_ref[:, cols]).astype(BF)
+        squares = scales[rows, :] + gained(c, 1 - core)
+        scales[rows, :] = lax.rsqrt(squares * (1.0 / 8192) + norm_eps)
 
     def stage_w(n):
         if n == 0:
@@ -297,7 +306,7 @@
                 wide_w[...] = source[2 * at : 2 * at + 1024, :].astype(F32)
                 for e in range(2):
                     cols = slice((2 * which + e) * 128, (2 * which + e + 1) * 128)
-                    w_all[at : at + 512, cols] = wide_w[pl.ds(e, 512, stride=2), :].astype(BF)
+                    w_all[part, n * 512 : n * 512 + 512, cols] = wide_w[pl.ds(e, 512, stride=2), :].astype(BF)
 
     def stage_r(_):
         lane = lax.broadcasted_iota(jnp.int32, (64, 128), 1)
@@ -308,14 +317,26 @@
         cosine[...] = jnp.cos(angles)
         sine[...] = jnp.where(lane < 64, -1.0, 1.0) * jnp.sin(angles)
 
-    def stage_t(_):
+    def project(which, total):
         def step(i, total):
             cols = pl.ds(pl.multiple_of(i * 1024, 1024), 1024)
             return total + jnp.dot(
-                normed[:, cols], w_all[cols, :], preferred_element_type=F32
+                normed[which, :, cols], w_all[which, cols, :], preferred_element_type=F32
             )
 
-        total = lax.fori_loop(0, 8, step, jnp.zeros((64, 512), F32))
+        return lax.fori_loop(0, 4, step, total)
+
+    def stage_u(_):
+        projected[...] = project(core, jnp.zeros((64, 512), F32))
+
+    def stage_s(n):
+        for c in range(CHUNKS):
+            for kind in range(KINDS):
+                if (n == 0) == (c < CHUNKS - 1 or kind not in (G, GF)):
+                    sent(kind, c)
+
+    def stage_t(_):
+        total = project(1 - core, projected[...]) * scales[:, :1]
 
         def rotated(value):
             return (value * cosine[...] + pltpu.roll(value, 64, 1) * sine[...]).astype(BF)
@@ -355,7 +376,6 @@
     loads[1].wait()
     for load in loads[2:]:
         load.start()
-    pl.semaphore_wait(barrier, len(everyone))
     stages = dict(
         a=stage_a,
         b=stage_b,
@@ -369,6 +389,8 @@
         i=stage_i,
         w=stage_w,
         r=stage_r,
+        u=stage_u,
+        s=stage_s,
         t=stage_t,
     )
     waited = False
@@ -377,10 +399,6 @@
             loads[2].wait()
             waited = True
         stages[step[0]](int(step[1]))
-
-    for c in range(CHUNKS):
-        for kind in range(KINDS):
-            sent(kind, c)
 
 
 def hand_over(mixed_in, attended_in, mixed_out, attended_out):
@@ -429,10 +447,12 @@
             pltpu.VMEM((2, 1024, 128), BF),
             pltpu.VMEM((1024, 128), F32),
             pltpu.VMEM((128, 128), F32),
-            pltpu.VMEM((8192, 512), BF),
-            pltpu.VMEM((64, 8192), BF),
+            pltpu.VMEM((2, 4096, 512), BF),
+            pltpu.VMEM((2, 64, 4096), BF),
             pltpu.VMEM((64, 128), F32),
             pltpu.VMEM((64, 128), F32),
+            pltpu.VMEM((64, 128), F32),
+            pltpu.VMEM((64, 512), F32),
             pltpu.SemaphoreType.DMA((6,)),
             pltpu.SemaphoreType.DMA((KINDS, CHUNKS)),
             pltpu.SemaphoreType.DMA((KINDS, CHUNKS)),

time: 68.5 us -> 66.3 us (0.968)
  Pallas kernels: 67 us -> 64.8 us
    pallas_call x1, Pallas kernels: 65.6 us -> 63.3 us  [ffn_block(): pl.pallas_call(ffn_kernel, out_shape=(jax.ShapeDtypeStruct((64, 512), BF)...]
where the time goes in v4:
time: 66.3 us; the launch traced here: 66.1 us
  Pallas kernels  64.8 us (98%)
  between operations  1.29 us (2%)
    pallas_call x1, Pallas kernels, ffn_block(): pl.pallas_call(ffn_kernel, out_shape=(jax.ShapeDtypeStruct((64, 512), BF)...  63.3 us
    pallas_call x1, Pallas kernels, ffn_block(): pl.pallas_call(hand_over, out_shape=(jax.ShapeDtypeStruct((64, 512), BF),...  1.48 us

profile of v4, /device:TPU:1, one launch (start us, length us, event | category | flops | bytes accessed | tf_op | source)
XLA Modules:
  0.0 66.1 jit_solution(10371795741518582630)
XLA Ops:
  1.3 63.3 %ffn_block.1 = (bf16[64,512]{1,0:T(8,128)(2,1)}, bf16[128,128]{1,0:T(8,128)(2,1)}) custom-call(bf16[8,2,64,512]{3,2,1,0:T(8,128)(2,1)} %bitcast.10, bf16[2,512,896]{2,1,0:T(8,128)(2,1)} %wgu_hbm.1, bf16[896,512]{1,0:T(8,128)(2,1)} %wd_hbm.1, bf16[64,512]{1,0:T(8,128)(2,1)} %stream_ref.1, f32[1,8192]{1,0:T(1,128)} %bitcast.12, bf16[16384,128]{1,0:T(8,128)(2,1)} %bitcast.8, ...), custom_call_target="tpu_custom_call" | custom-call | tf_op jit(solution)/shard_map/ffn_block/pallas_call | solution.py:413
  64.6 1.5 %hand_over.1 = (bf16[64,512]{1,0:T(8,128)(2,1)}, bf16[128,128]{1,0:T(8,128)(2,1)}) custom-call(bf16[64,512]{1,0:T(8,128)(2,1)} %get-tuple-element.6.mixed_in, bf16[128,128]{1,0:T(8,128)(2,1)} %get-tuple-element.7.attended_in), custom_call_target="tpu_custom_call" | custom-call | tf_op jit(solution)/shard_map/hand_over/pallas_call | solution.py:475

commit v5 on v4

--- a/solution.py
+++ b/solution.py
@@ -37,8 +37,8 @@
     x_hbm,
     wgu_hbm,
     wd_hbm,
-    stream_ref,
-    gain_ref,
+    stream_hbm,
+    gain_hbm,
     wq_hbm,
     wkv_hbm,
     cache_hbm,
@@ -75,6 +75,8 @@
     spread,
     w_all,
     normed,
+    stream_ref,
+    gain_ref,
     cosine,
     sine,
     scales,
@@ -96,17 +98,21 @@
         pltpu.make_async_copy(src, dst, load_sem.at[i])
         for i, (src, dst) in enumerate(
             (
-                (x_hbm, x_v),
-                (wgu_hbm, wgu_v),
+                (x_hbm.at[:, :, 0:ROWS], x_v.at[:, :, 0:ROWS]),
+                (wgu_hbm.at[0], wgu_v.at[0]),
+                (wgu_hbm.at[1], wgu_v.at[1]),
+                (x_hbm.at[:, :, ROWS:], x_v.at[:, :, ROWS:]),
                 (wd_hbm, wd_v),
                 (wq_hbm, wq_v),
                 (wkv_hbm, wkv_v),
                 (cache_hbm, cache_v),
+                (stream_hbm, stream_ref),
+                (gain_hbm, gain_ref),
             )
         )
     ]
-    loads[0].start()
-    loads[1].start()
+    for load in loads[:4]:
+        load.start()
 
     def y_peer(dy):
         y2 = (y + dy) % 4
@@ -163,22 +169,26 @@
     def sent(kind, c):
         wait_bytes(arrivals(kind, c), send_sem.at[kind, c])
 
-    def gate_up(rows, c):
+    def gate_up(rows, c, e):
         left = x_v[:, rows, pl.ds(c * ROWS, ROWS), :].reshape(CHIPS * ROWS, 512)
-        return [
-            jnp.dot(left, wgu_v[e], preferred_element_type=F32).reshape(CHIPS, ROWS, 896)
-            for e in range(2)
-        ]
+        return jnp.dot(left, wgu_v[e], preferred_element_type=F32).reshape(CHIPS, ROWS, 896)
 
     def stage_a(c):
-        for e, part in enumerate(gate_up(1 - core, c)):
+        for e in range(2):
+            if c == 0:
+                if e == 0:
+                    loads[0].wait()
+                loads[1 + e].wait()
+            part = gate_up(1 - core, c, e)
             core_send[c, :, :, e * 896 : (e + 1) * 896] = part.astype(BF)
         if c == 0:
             pl.semaphore_wait(barrier, len(everyone))
+            for load in loads[4:]:
+                load.start()
         send(core_send.at[c], core_recv.at[c], CORE, c, sibling)
 
     def stage_b(c):
-        parts = gate_up(core, c)
+        parts = [gate_up(core, c, e) for e in range(2)]
         arrived(CORE, c)
         for e, part in enumerate(parts):
             total = part + core_recv[c, :, :, e * 896 : (e + 1) * 896].astype(F32)
@@ -276,13 +286,16 @@
 
     def gained(c, which):
         rows = slice(c * ROWS, (c + 1) * ROWS)
-        squares = jnp.zeros((ROWS, 1), F32)
-        for k in range(CHIPS):
+
+        def block(k, squares):
             wide = full_all[c, k, which].astype(F32)
             gain = gain_ref[:, pl.ds(pl.multiple_of((k * 2 + which) * 512, 512), 512)]
-            squares = squares + jnp.sum(wide * wide, axis=1, keepdims=True)
-            normed[which, rows, k * 512 : (k + 1) * 512] = (wide * gain).astype(BF)
-        return squares
+            cols = pl.ds(pl.multiple_of(k * 512, 512), 512)
+            normed[which, rows, cols] = (wide * gain).astype(BF)
+            return squares + wide * wide
+
+        squares = lax.fori_loop(0, CHIPS, block, jnp.zeros((ROWS, 512), F32))
+        return jnp.sum(squares, axis=1, keepdims=True)
 
     def stage_h(c):
         arrived(G, c)
@@ -298,15 +311,21 @@
 
     def stage_w(n):
         if n == 0:
-            loads[3].wait()
-            loads[4].wait()
-        for which, source in enumerate((wq_v, wkv_v)):
-            for part in range(2):
-                at = n * 1024 + part * 512
-                wide_w[...] = source[2 * at : 2 * at + 1024, :].astype(F32)
+            loads[5].wait()
+            loads[6].wait()
+
+        def piece(i, _):
+            part, at = i // 4, i % 4 * 128
+            rows = pl.ds(pl.multiple_of(n * 2048 + i * 256, 256), 256)
+            for which, source in enumerate((wq_v, wkv_v)):
+                wide_w[which] = source[rows, :].astype(F32)
                 for e in range(2):
                     cols = slice((2 * which + e) * 128, (2 * which + e + 1) * 128)
-                    w_all[part, n * 512 : n * 512 + 512, cols] = wide_w[pl.ds(e, 512, stride=2), :].astype(BF)
+                    into = pl.ds(pl.multiple_of(n * 512 + at, 128), 128)
+                    w_all[part, into, cols] = wide_w[which, pl.ds(e, 128, stride=2), :].astype(BF)
+            return 0
+
+        lax.fori_loop(0, 8, piece, 0)
 
     def stage_r(_):
         lane = lax.broadcasted_iota(jnp.int32, (64, 128), 1)
@@ -344,7 +363,7 @@
         queries = jnp.concatenate([rotated(total[:, :128]), rotated(total[:, 128:256])], axis=0)
         k_new = rotated(total[:, 256:384])
         v_new = total[:, 384:].astype(BF)
-        loads[5].wait()
+        loads[7].wait()
         head_scale = 128 ** (-0.5)
         dims = (((1,), (1,)), ((), ()))
         cache_scores = (
@@ -364,18 +383,15 @@
         denominator = jnp.sum(cache_exp, axis=1, keepdims=True) + jnp.sum(
             own_exp, axis=1, keepdims=True
         )
-        cache_w = (cache_exp / denominator).astype(BF)
-        own_w = (own_exp / denominator).astype(BF)
+        inverse = 1.0 / denominator
+        cache_w = (cache_exp * inverse).astype(BF)
+        own_w = (own_exp * inverse).astype(BF)
         result = jnp.dot(cache_w, cache_v[1], preferred_element_type=F32)
         result = result + jnp.dot(own_w, v_new, preferred_element_type=F32)
         for g in range(2):
             spread[pl.ds(g, 64, stride=2), :] = result[g * 64 : (g + 1) * 64]
         attended_ref[...] = spread[...].astype(BF)
 
-    loads[0].wait()
-    loads[1].wait()
-    for load in loads[2:]:
-        load.start()
     stages = dict(
         a=stage_a,
         b=stage_b,
@@ -393,11 +409,10 @@
         s=stage_s,
         t=stage_t,
     )
-    waited = False
+    first_use = {"a1": 3, "e0": 4, "g0": 8, "h0": 9}
     for step in ORDER:
-        if step[0] == "e" and not waited:
-            loads[2].wait()
-            waited = True
+        if step in first_use:
+            loads[first_use[step]].wait()
         stages[step[0]](int(step[1]))
 
 
@@ -416,7 +431,7 @@
             jax.ShapeDtypeStruct((64, 512), BF),
             jax.ShapeDtypeStruct((128, 128), BF),
         ),
-        in_specs=[hbm, hbm, hbm, vmem, vmem, hbm, hbm, hbm, smem],
+        in_specs=[hbm, hbm, hbm, hbm, hbm, hbm, hbm, hbm, smem],
         out_specs=(vmem, vmem),
         scratch_shapes=[
             pltpu.VMEM((CHIPS, 2, 64, 512), BF),
@@ -445,15 +460,17 @@
             pltpu.VMEM((16384, 128), BF),
             pltpu.VMEM((16384, 128), BF),
             pltpu.VMEM((2, 1024, 128), BF),
-            pltpu.VMEM((1024, 128), F32),
+            pltpu.VMEM((2, 256, 128), F32),
             pltpu.VMEM((128, 128), F32),
             pltpu.VMEM((2, 4096, 512), BF),
             pltpu.VMEM((2, 64, 4096), BF),
+            pltpu.VMEM((64, 512), BF),
+            pltpu.VMEM((1, 8192), F32),
             pltpu.VMEM((64, 128), F32),
             pltpu.VMEM((64, 128), F32),
             pltpu.VMEM((64, 128), F32),
             pltpu.VMEM((64, 512), F32),
-            pltpu.SemaphoreType.DMA((6,)),
+            pltpu.SemaphoreType.DMA((10,)),
             pltpu.SemaphoreType.DMA((KINDS, CHUNKS)),
             pltpu.SemaphoreType.DMA((KINDS, CHUNKS)),
         ],

time: 66.3 us -> 65.7 us (level)
  no operation moved by 1% of the time
where the time goes in v5:
time: 65.7 us; the launch traced here: 65.6 us
  Pallas kernels  64.3 us (98%)
  between operations  1.29 us (2%)
    pallas_call x1, Pallas kernels, ffn_block(): pl.pallas_call(ffn_kernel, out_shape=(jax.ShapeDtypeStruct((64, 512), BF)...  62.8 us
    pallas_call x1, Pallas kernels, ffn_block(): pl.pallas_call(hand_over, out_shape=(jax.ShapeDtypeStruct((64, 512), BF),...  1.48 us

profile of v5, /device:TPU:1, one launch (start us, length us, event | category | flops | bytes accessed | tf_op | source)
XLA Modules:
  0.0 65.6 jit_solution(8346362417188475283)
XLA Ops:
  1.3 62.8 %ffn_block.1 = (bf16[64,512]{1,0:T(8,128)(2,1)}, bf16[128,128]{1,0:T(8,128)(2,1)}) custom-call(bf16[8,2,64,512]{3,2,1,0:T(8,128)(2,1)} %bitcast.10, bf16[2,512,896]{2,1,0:T(8,128)(2,1)} %wgu_hbm.1, bf16[896,512]{1,0:T(8,128)(2,1)} %wd_hbm.1, bf16[64,512]{1,0:T(8,128)(2,1)} %stream_hbm.1, f32[1,8192]{1,0:T(1,128)} %bitcast.12, bf16[16384,128]{1,0:T(8,128)(2,1)} %bitcast.8, ...), custom_call_target="tpu_custom_call" | custom-call | tf_op jit(solution)/shard_map/ffn_block/pallas_call | solution.py:428
  64.1 1.5 %hand_over.1 = (bf16[64,512]{1,0:T(8,128)(2,1)}, bf16[128,128]{1,0:T(8,128)(2,1)}) custom-call(bf16[64,512]{1,0:T(8,128)(2,1)} %get-tuple-element.6.mixed_in, bf16[128,128]{1,0:T(8,128)(2,1)} %get-tuple-element.7.attended_in), custom_call_target="tpu_custom_call" | custom-call | tf_op jit(solution)/shard_map/hand_over/pallas_call | solution.py:492
